TPU v7x, 128 devices: a whole 4x4x4 slice. The times are simulated.
128 devices in a mesh: node: 16 (over y, z), chan: 8 (over x, core).
Axes of the slice: x: 4, y: 4, z: 4, core: 2. Of those that a mesh axis runs over, the one named last changes fastest.
Arguments:
- latents: bfloat16 [12288, 1024], P('node', 'chan'), may hold values from -6 to 6
- edge_attr: bfloat16 [24576, 1024], P('node', 'chan'), may hold values from -6 to 6
- edge_src: int32 [24576], P('node'), may hold values from 0 to 4863, as said below
- edge_dst: int32 [24576], P('node'), may hold values from 0 to 767
- send_blocks: int32 [16, 16, 2], P('node'), may hold values from 0 to 5
- edge_hidden_w: bfloat16 [3072, 1024], P(None, 'chan'), may hold values from -0.109375 to 0.109375
- edge_out_w: bfloat16 [1024, 1024], P('chan'), may hold values from -0.1875 to 0.1875
- node_hidden_w: bfloat16 [2048, 1024], P(None, 'chan'), may hold values from -0.125 to 0.125
- node_out_w: bfloat16 [1024, 1024], P('chan'), may hold values from -0.1875 to 0.1875
- node_cotangent: bfloat16 [12288, 1024], P('node', 'chan'), may hold values from -6 to 6
- edge_cotangent: bfloat16 [24576, 1024], P('node', 'chan'), may hold values from -6 to 6
Outputs:
- grad_latents: float32 [12288, 1024], P('node', 'chan')
- grad_edges: float32 [24576, 1024], P('node', 'chan')
- grad_edge_hidden: float32 [3072, 1024], P('node', 'chan')
- grad_edge_out: float32 [1024, 1024], P('chan', 'node')
- grad_node_hidden: float32 [2048, 1024], P('node', 'chan')
- grad_node_out: float32 [1024, 1024], P('chan', 'node')
Inputs may be any that keep to these rules, and one draw needn't show every extreme that they name: `edge_src`: On each node device half of the edges have a source among its own nodes and half in its halo table, and every halo slot (p, s) is the source of exactly 24 of its edges. send_blocks[p, q, s] is the block of node device p that device q holds as halo slot s.
All inputs are finite; a program needn't handle non-finite values.
Results may differ from a plain program's by a relative error of at most 0.025.
Values may be sent and summed in bfloat16 or wider, within the bound.
A program may use at most 192 MiB of HBM per device.

v0:
```python
import jax
import jax.numpy as jnp
from jax import lax
from jax.sharding import PartitionSpec as P

BLOCK = 128


def silu_grad(value):
    sig = jax.nn.sigmoid(value)
    return sig * (1.0 + value * (1.0 - sig))


def on_device(
    latents,
    edge_attr,
    edge_src,
    edge_dst,
    send_blocks,
    edge_hidden_w,
    edge_out_w,
    node_hidden_w,
    node_out_w,
    node_cotangent,
    edge_cotangent,
):
    devices = lax.axis_size("node")
    nodes_here = latents.shape[0]
    edges_here = edge_attr.shape[0]
    slice_width = latents.shape[1]
    edge_scale = float(edges_here * devices) ** (-0.5)
    node_scale = float(nodes_here * devices) ** (-0.5)
    requested = send_blocks[0]
    latent_full, edge_full, cot_full = (
        lax.all_gather(latents, "chan", axis=1, tiled=True),
        lax.all_gather(edge_attr, "chan", axis=1, tiled=True),
        lax.all_gather(node_cotangent, "chan", axis=1, tiled=True),
    )
    full_width = latent_full.shape[1]
    outgoing = latent_full.reshape(-1, BLOCK, full_width)[requested]
    incoming = lax.all_to_all(outgoing, "node", split_axis=0, concat_axis=0, tiled=True)
    table = jnp.concatenate([latent_full, incoming.reshape(-1, full_width)], axis=0)
    table_size = table.shape[0]
    edge_inputs = jnp.concatenate([table[edge_src], latent_full[edge_dst], edge_full], axis=1)
    hidden_pre = jnp.dot(edge_inputs, edge_hidden_w, preferred_element_type=jnp.float32)
    hidden = jax.nn.silu(hidden_pre).astype(jnp.bfloat16)
    message_terms = jnp.dot(hidden, edge_out_w, preferred_element_type=jnp.float32)
    messages = lax.psum_scatter(
        message_terms.astype(jnp.bfloat16), "chan", scatter_dimension=1, tiled=True
    ).astype(jnp.float32)
    new_edges = (edge_attr.astype(jnp.float32) + messages).astype(jnp.bfloat16)
    node_sum = jax.ops.segment_sum(
        new_edges.astype(jnp.float32), edge_dst, num_segments=nodes_here
    ).astype(jnp.bfloat16)
    sum_full = lax.all_gather(node_sum, "chan", axis=1, tiled=True)
    node_inputs = jnp.concatenate([latent_full, sum_full], axis=1)
    node_pre = jnp.dot(node_inputs, node_hidden_w, preferred_element_type=jnp.float32)
    node_hidden = jax.nn.silu(node_pre).astype(jnp.bfloat16)
    term_node_out = node_scale * jnp.dot(
        node_hidden.T, cot_full, preferred_element_type=jnp.float32
    )
    node_hidden_grad = (
        jnp.dot(cot_full, node_out_w.T, preferred_element_type=jnp.float32) * silu_grad(node_pre)
    ).astype(jnp.bfloat16)
    term_node_hidden = node_scale * jnp.dot(
        node_inputs.T, node_hidden_grad, preferred_element_type=jnp.float32
    )
    node_terms = jnp.dot(
        node_hidden_grad, node_hidden_w.T, preferred_element_type=jnp.float32
    ).reshape(nodes_here, 2, -1)
    node_input_grad = lax.psum_scatter(
        node_terms.astype(jnp.bfloat16), "chan", scatter_dimension=2, tiled=True
    ).astype(jnp.float32)
    target_share = node_input_grad[:, 1]
    edge_total = edge_cotangent.astype(jnp.float32) + target_share[edge_dst]
    message_grad = edge_total.astype(jnp.bfloat16)
    message_full = lax.all_gather(message_grad, "chan", axis=1, tiled=True)
    term_edge_out = edge_scale * jnp.dot(hidden.T, message_full, preferred_element_type=jnp.float32)
    edge_hidden_grad = (
        jnp.dot(message_full, edge_out_w.T, preferred_element_type=jnp.float32)
        * silu_grad(hidden_pre)
    ).astype(jnp.bfloat16)
    term_edge_hidden = edge_scale * jnp.dot(
        edge_inputs.T, edge_hidden_grad, preferred_element_type=jnp.float32
    )
    edge_terms = jnp.dot(
        edge_hidden_grad, edge_hidden_w.T, preferred_element_type=jnp.float32
    ).reshape(edges_here, 3, -1)
    edge_input_grad = lax.psum_scatter(
        edge_terms.astype(jnp.bfloat16), "chan", scatter_dimension=2, tiled=True
    ).astype(jnp.float32)
    grad_edges = edge_total + edge_input_grad[:, 2]
    source_sum = jax.ops.segment_sum(edge_input_grad[:, 0], edge_src, num_segments=table_size)
    node_grads = node_cotangent.astype(jnp.float32) + node_input_grad[:, 0]
    node_grads = node_grads + jax.ops.segment_sum(
        edge_input_grad[:, 1], edge_dst, num_segments=nodes_here
    )
    node_grads = node_grads + source_sum[:nodes_here]
    halo_sum = source_sum[nodes_here:]
    returned = halo_sum.reshape(devices, -1, BLOCK, slice_width).astype(jnp.bfloat16)
    arrived = lax.all_to_all(returned, "node", split_axis=0, concat_axis=0, tiled=True)
    node_blocks = node_grads.reshape(-1, BLOCK, slice_width)
    node_blocks = node_blocks.at[requested.reshape(-1)].add(
        arrived.reshape(-1, BLOCK, slice_width).astype(jnp.float32)
    )
    node_grads = node_blocks.reshape(nodes_here, slice_width)
    grad_eh, grad_eo, grad_nh, grad_no = (
        lax.psum_scatter(
            term_edge_hidden.astype(jnp.bfloat16), "node", scatter_dimension=0, tiled=True
        ).astype(jnp.float32),
        lax.psum_scatter(
            term_edge_out.astype(jnp.bfloat16), "node", scatter_dimension=1, tiled=True
        ).astype(jnp.float32),
        lax.psum_scatter(
            term_node_hidden.astype(jnp.bfloat16), "node", scatter_dimension=0, tiled=True
        ).astype(jnp.float32),
        lax.psum_scatter(
            term_node_out.astype(jnp.bfloat16), "node", scatter_dimension=1, tiled=True
        ).astype(jnp.float32),
    )
    return (node_grads, grad_edges, grad_eh, grad_eo, grad_nh, grad_no)


def solution(mesh):
    return jax.shard_map(
        on_device,
        mesh=mesh,
        in_specs=(
            P("node", "chan"),
            P("node", "chan"),
            P("node"),
            P("node"),
            P("node", None, None),
            P(None, "chan"),
            P("chan", None),
            P(None, "chan"),
            P("chan", None),
            P("node", "chan"),
            P("node", "chan"),
        ),
        out_specs=(
            P("node", "chan"),
            P("node", "chan"),
            P("node", "chan"),
            P("chan", "node"),
            P("node", "chan"),
            P("chan", "node"),
        ),
        check_vma=False,
    )
```

profile of v0, /device:TPU:0, one launch (start us, length us, event | category | flops | bytes accessed | tf_op | source)
XLA Modules:
  0.0 885.5 jit_solution(6447226370324369325)
XLA Ops:
  8.8 28.5 %all-gather.8.cloned.1.call-done = bf16[768,1024]{1,0:T(8,128)(2,1)} async-done(((bf16[768,128]{1,0:T(8,128)(2,1)}), bf16[768,1024]{1,0:T(8,128)(2,1)}) %all-gather.8.cloned.1.call-update) | async-done | bytes 1572880 | tf_op jit(solution)/shard_map/all_gather | solution.py:35
  37.3 6.4 gather_fusion
  43.8 7.1 all-to-all-start
  51.8 5.8 gather_fusion.2
  57.6 140.1 %all-to-all-done = bf16[16,2,128,1024]{3,2,1,0:T(8,128)(2,1)} async-done(((bf16[16,2,128,1024]{3,2,1,0:T(8,128)(2,1)}), bf16[16,2,128,1024]{3,2,1,0:T(8,128)(2,1)}, u32[]{:S(2)}, u32[]{:S(2)}) %all-to-all-start) | async-done | bytes 8388640 | tf_op jit(solution)/shard_map/all_to_all | solution.py:41
  197.7 8.4 pad_maximum_fusion
  206.0 12.9 %gather_fusion.1 = bf16[1536,1024]{1,0:T(8,128)(2,1)} fusion(bf16[4864,1024]{1,0:T(8,128)(2,1)} %pad_maximum_fusion, s32[2048]{0:T(1024)S(1)} %pad_clamp_fusion.1), kind=kCustom, calls=%fused_computation.1 | custom fusion | bytes 6297600 | tf_op jit(solution)/shard_map/gather | solution.py:44
  219.0 4.1 constant_dynamic-update-slice_fusion.2
  223.1 2.0 constant_dynamic-update-slice_fusion.1
  225.1 4.0 constant_dynamic-update-slice_fusion
  229.1 5.2 fusion.18
  234.3 2.7 convolution_convert_fusion.1
  237.0 4.6 copy.31
  241.7 42.0 %reduce-scatter.22.cloned.1.call-done = bf16[128,1536]{1,0:T(8,128)(2,1)} async-done(((bf16[1024,1536]{1,0:T(8,128)(2,1)}), bf16[128,1536]{1,0:T(8,128)(2,1)}) %reduce-scatter.22.cloned.1.call-update) | async-done | bytes 393232
  283.8 1.2 copy.32
  285.0 9.0 %scatter_custom_fusion = f32[768,128]{1,0:T(8,128)S(1)} fusion(s32[1536]{0:T(1024)} %param.14, bf16[1536,128]{1,0:T(8,128)(2,1)S(1)} %copy.32, bf16[1536,128]{1,0:T(8,128)(2,1)S(1)} %copy-done.7, f32[]{:T(128)} %constant.9.clone.1), kind=kCustom, calls=%fused_computation.34 | custom fusion | flops 1179648 | bytes 1180160 | tf_op jit(solution)/shard_map/scatter-add | solution.py:52
  294.0 0.7 convert_element_type.98
  295.6 1.3 constant_dynamic-update-slice_fusion.4
  296.9 21.9 %all-gather.12.cloned.1.call-done = bf16[768,1024]{1,0:T(8,128)(2,1)} async-done(((bf16[768,128]{1,0:T(8,128)(2,1)}), bf16[768,1024]{1,0:T(8,128)(2,1)}) %all-gather.12.cloned.1.call-update) | async-done | bytes 1572880 | tf_op jit(solution)/shard_map/all_gather | solution.py:55
  318.8 2.8 constant_dynamic-update-slice_fusion.3
  321.6 2.9 fusion.19
  324.5 22.0 %all-gather.6.cloned.1.call-done = bf16[768,1024]{1,0:T(8,128)(2,1)} async-done(((bf16[768,128]{1,0:T(8,128)(2,1)}), bf16[768,1024]{1,0:T(8,128)(2,1)}) %all-gather.6.cloned.1.call-update) | async-done | bytes 1572880 | tf_op jit(solution)/shard_map/all_gather | solution.py:37
  346.5 2.0 fusion.7
  348.5 2.6 convolution_convert_fusion.2
  351.1 6.1 convert_element_type.101
  357.2 11.1 %copy.33 = bf16[768,2,1024]{0,1,2:T(2,128)(2,1)} copy(bf16[768,2,1024]{2,1,0:T(2,128)(2,1)} %convert_element_type.101) | data formatting | bytes 6291456
  368.4 4.1 copy.39
  372.5 36.7 %reduce-scatter.24.cloned.1.call-done = bf16[128,1536]{1,0:T(8,128)(2,1)} async-done(((bf16[1024,1536]{1,0:T(8,128)(2,1)}), bf16[128,1536]{1,0:T(8,128)(2,1)}) %reduce-scatter.24.cloned.1.call-update) | async-done | bytes 393232
  409.3 1.1 reshape.168
  410.9 0.9 copy-done.5
  411.9 2.6 gather_fusion.3
  414.5 0.9 fusion.12
  415.5 30.6 %all-gather.14.cloned.1.call-done = bf16[1536,1024]{1,0:T(8,128)(2,1)} async-done(((bf16[1536,128]{1,0:T(8,128)(2,1)}), bf16[1536,1024]{1,0:T(8,128)(2,1)}) %all-gather.14.cloned.1.call-update) | async-done | bytes 3145744 | tf_op jit(solution)/shard_map/all_gather | solution.py:77
  446.1 3.1 fusion.1
  449.2 5.3 convolution_convert_fusion
  454.5 12.6 %copy.28 = bf16[1536,3072]{0,1:T(8,128)(2,1)} copy(bf16[1536,3072]{1,0:T(8,128)(2,1)} %convolution_convert_fusion) | data formatting | bytes 18874368 | tf_op jit(solution)/shard_map/convert_element_type | solution.py:90
  467.1 14.8 %copy.35 = bf16[1536,3,1024]{0,1,2:T(4,128)(2,1)} copy(bf16[1536,3,1024]{0,2,1:T(8,128)(2,1)} %bitcast.68) | data formatting | bytes 18874368
  481.8 11.4 %copy.40 = bf16[128,8,3,1536]{3,1,2,0:T(8,128)(2,1)} copy(bf16[128,8,3,1536]{3,2,1,0:T(4,128)(2,1)} %bitcast.66) | data formatting | bytes 18874368
  493.5 1.1 copy-done.12
  494.6 1.4 fusion.6
  496.1 3.8 fusion.2
  500.0 3.9 fusion.5
  504.0 7.3 fusion
  511.5 40.3 %reduce-scatter.26.cloned.1.call-done = bf16[128,4608]{1,0:T(8,128)(2,1)} async-done(((bf16[1024,4608]{1,0:T(8,128)(2,1)}), bf16[128,4608]{1,0:T(8,128)(2,1)}) %reduce-scatter.26.cloned.1.call-update) | async-done | bytes 1179664
  551.8 2.6 reshape.170
  554.4 2.3 copy.36
  556.6 1.4 convert_element_type.108
  558.1 10.4 %scatter_custom_fusion.1 = f32[4864,128]{1,0:T(8,128)} fusion(s32[1536]{0:T(1024)S(1)} %copy-done.9, f32[]{:T(128)} %constant.9.clone.1, f32[1536,3,128]{2,0,1:T(8,128)S(1)} %convert_element_type.108), kind=kCustom, calls=%fused_computation.19 | custom fusion | flops 196608 | bytes 3276804 | tf_op jit(solution)/shard_map/scatter-add | solution.py:93
  568.4 2.7 slice.59
  571.1 7.0 all-to-all-start.1
  578.1 55.5 %reduce-scatter.20.cloned.1.call-done = bf16[128,64]{0,1:T(8,128)(2,1)} async-done(((bf16[128,1024]{0,1:T(8,128)(2,1)}), bf16[128,64]{0,1:T(8,128)(2,1)}) %reduce-scatter.20.cloned.1.call-update) | async-done | bytes 16400 | tf_op jit(solution)/shard_map/reduce_scatter | solution.py:117
  633.6 1.3 convert_element_type.120
  634.9 73.7 %reduce-scatter.18.cloned.1.call-done = bf16[128,128]{1,0:T(8,128)(2,1)} async-done(((bf16[2048,128]{1,0:T(8,128)(2,1)}), bf16[128,128]{1,0:T(8,128)(2,1)}) %reduce-scatter.18.cloned.1.call-update) | async-done | bytes 32784 | tf_op jit(solution)/shard_map/reduce_scatter | solution.py:114
  708.7 1.4 convert_element_type.117
  710.1 73.8 %reduce-scatter.16.cloned.1.call-done = bf16[128,64]{0,1:T(8,128)(2,1)} async-done(((bf16[128,1024]{0,1:T(8,128)(2,1)}), bf16[128,64]{0,1:T(8,128)(2,1)}) %reduce-scatter.16.cloned.1.call-update) | async-done | bytes 16400 | tf_op jit(solution)/shard_map/reduce_scatter | solution.py:111
  783.8 1.3 convert_element_type.115
  785.2 74.6 %reduce-scatter.14.cloned.1.call-done = bf16[192,128]{1,0:T(8,128)(2,1)} async-done(((bf16[3072,128]{1,0:T(8,128)(2,1)}), bf16[192,128]{1,0:T(8,128)(2,1)}) %reduce-scatter.14.cloned.1.call-update) | async-done | bytes 49168 | tf_op jit(solution)/shard_map/reduce_scatter | solution.py:108
  859.8 1.4 convert_element_type.113
  861.3 1.2 slice_add_fusion
  862.5 9.1 %scatter_custom_fusion.2 = f32[768,128]{1,0:T(8,128)S(1)} fusion(f32[768,128]{1,0:T(8,128)S(1)} %slice_add_fusion, s32[1536]{0:T(1024)} %param.14, f32[1536,3,128]{2,0,1:T(8,128)S(1)} %convert_element_type.108), kind=kCustom, calls=%fused_computation.31 | custom fusion | flops 196608 | bytes 1179648 | tf_op jit(solution)/shard_map/scatter-add | solution.py:95
  871.6 2.2 fusion.8
  873.8 1.5 bitcast_convert_fusion
  875.2 2.7 scatter_fusion
  877.9 0.7 copy-done.2
  (73 shorter events, 4.7 us)
Async XLA Ops:
  7.2 221.9 %copy-start = (bf16[3072,128]{1,0:T(8,128)(2,1)S(1)}, bf16[3072,128]{1,0:T(8,128)(2,1)}, u32[]{:S(2)}) copy-start(bf16[3072,128]{1,0:T(8,128)(2,1)} %param.16) | copy-start | bytes 2359300
  7.2 30.1 %all-gather.8.cloned.1.call-start = ((), (), s32[]{:S(2)}) async-start(), calls=%async_computation.10 | async-start | bytes 1769472 | tf_op jit(solution)/shard_map/all_gather | solution.py:35
  43.8 7.9 copy-start.9
  43.8 8.0 copy-start.10
  43.8 8.0 copy-start.1
  43.8 153.9 %all-to-all-start = ((bf16[16,2,128,1024]{3,2,1,0:T(8,128)(2,1)}), bf16[16,2,128,1024]{3,2,1,0:T(8,128)(2,1)}, u32[]{:S(2)}, u32[]{:S(2)}) async-start(bf16[16,2,128,1024]{3,2,1,0:T(8,128)(2,1)} %bitcast.69), calls=%async_computation | async-start | bytes 16777216 | tf_op jit(solution)/shard_map/all_to_all | solution.py:41
  50.9 174.2 %all-gather.10.cloned.1.call-start = ((), (), s32[]{:S(2)}) async-start(), calls=%async_computation.11 | async-start | bytes 3538944 | tf_op jit(solution)/shard_map/all_gather | solution.py:36
  51.6 232.1 %reduce-scatter.22.cloned.1.call-start = ((), (), s32[]{:S(2)}) async-start(), calls=%async_computation.18 | async-start | bytes 3538944
  219.0 4.1 copy-start.3
  229.1 5.2 copy-start.14
  234.3 2.7 copy-start.16
  241.7 43.3 %copy-start.7 = (bf16[1536,128]{1,0:T(8,128)(2,1)S(1)}, bf16[1536,128]{1,0:T(8,128)(2,1)}, u32[]{:S(2)}) copy-start(bf16[1536,128]{1,0:T(8,128)(2,1)} %param.12) | copy-start | bytes 1179652
  241.7 77.1 %all-gather.12.cloned.1.call-start = ((), (), s32[]{:S(2)}) async-start(), calls=%async_computation.12 | async-start | bytes 1769472 | tf_op jit(solution)/shard_map/all_gather | solution.py:55
  294.8 51.7 %all-gather.6.cloned.1.call-start = ((), (), s32[]{:S(2)}) async-start(), calls=%async_computation.9 | async-start | bytes 1769472 | tf_op jit(solution)/shard_map/all_gather | solution.py:37
  295.4 26.2 %copy-start.6 = (bf16[2048,128]{1,0:T(8,128)(2,1)S(1)}, bf16[2048,128]{1,0:T(8,128)(2,1)}, u32[]{:S(2)}) copy-start(bf16[2048,128]{1,0:T(8,128)(2,1)} %param.18) | copy-start | bytes 1572868
  295.4 113.9 %reduce-scatter.24.cloned.1.call-start = ((), (), s32[]{:S(2)}) async-start(), calls=%async_computation.19 | async-start | bytes 3538944
  321.6 24.9 %copy-start.13 = (bf16[128,1024]{1,0:T(8,128)(2,1)S(1)}, bf16[128,1024]{1,0:T(8,128)(2,1)}, u32[]{:S(2)}) copy-start(bf16[128,1024]{1,0:T(8,128)(2,1)} %param.19) | copy-start | bytes 786436
  372.5 73.6 %all-gather.14.cloned.1.call-start = ((), (), s32[]{:S(2)}) async-start(), calls=%async_computation.13 | async-start | bytes 3538944 | tf_op jit(solution)/shard_map/all_gather | solution.py:77
  410.9 0.9 copy-start.5
  411.8 2.6 copy-start.8
  411.9 34.2 %copy-start.15 = (bf16[128,1024]{1,0:T(8,128)(2,1)S(1)}, bf16[128,1024]{1,0:T(8,128)(2,1)}, u32[]{:S(2)}) copy-start(bf16[128,1024]{1,0:T(8,128)(2,1)} %param.17) | copy-start | bytes 786436
  414.5 34.7 %copy-start.4 = (f32[1536,128]{1,0:T(8,128)}, f32[1536,128]{1,0:T(8,128)S(1)}, u32[]{:S(2)}) copy-start(f32[1536,128]{1,0:T(8,128)S(1)} %gather_fusion.3) | copy-start | bytes 2359300
  415.4 136.3 %reduce-scatter.26.cloned.1.call-start = ((), (), s32[]{:S(2)}) async-start(), calls=%async_computation.20 | async-start | bytes 10616832
  493.2 1.4 copy-start.12
  493.2 140.4 %reduce-scatter.20.cloned.1.call-start = ((), (), s32[]{:S(2)}) async-start(), calls=%async_computation.17 | async-start | bytes 278528 | tf_op jit(solution)/shard_map/reduce_scatter | solution.py:117
  496.1 3.9 copy-start.17
  496.1 212.6 %reduce-scatter.18.cloned.1.call-start = ((), (), s32[]{:S(2)}) async-start(), calls=%async_computation.16 | async-start | bytes 557056 | tf_op jit(solution)/shard_map/reduce_scatter | solution.py:114
  499.9 283.9 %reduce-scatter.16.cloned.1.call-start = ((), (), s32[]{:S(2)}) async-start(), calls=%async_computation.15 | async-start | bytes 278528 | tf_op jit(solution)/shard_map/reduce_scatter | solution.py:111
  504.0 7.3 copy-start.11
  504.0 355.9 %reduce-scatter.14.cloned.1.call-start = ((), (), s32[]{:S(2)}) async-start(), calls=%async_computation.14 | async-start | bytes 835584 | tf_op jit(solution)/shard_map/reduce_scatter | solution.py:108
  571.1 302.7 %all-to-all-start.1 = ((bf16[16,2,128,128]{3,2,1,0:T(8,128)(2,1)}), bf16[16,2,128,128]{3,2,1,0:T(8,128)(2,1)}, u32[]{:S(2)}, u32[]{:S(2)}) async-start(bf16[16,2,128,128]{3,2,1,0:T(8,128)(2,1)} %bitcast.76), calls=%async_computation.1 | async-start | bytes 2097152 | tf_op jit(solution)/shard_map/all_to_all | solution.py:101
  877.9 0.7 copy-start.2
Sparse Core Ops, SparseCore 0:
  9.7 27.5 all-gather.7
  53.4 32.7 all-gather.9
  241.8 41.9 reduce-scatter.21
  294.9 23.8 all-gather.11
  320.3 26.1 all-gather.5
  372.6 36.6 reduce-scatter.23
  415.6 30.4 all-gather.13
  493.4 58.3 reduce-scatter.25
  555.0 78.5 reduce-scatter.19
  637.0 71.6 reduce-scatter.17
  712.4 71.3 reduce-scatter.15
  787.8 71.9 reduce-scatter.13
where the time goes:
time: 887 us; the launch traced here: 886 us
  waiting for transfers between devices  642 us (72%)
  local copies, waits for them, and re-layouts  120 us (14%)
  other arithmetic  53.7 us (6%)
  matrix products  40.1 us (5%)
  starting transfers between devices  15 us (2%)
  between operations  14.5 us (2%)
    all_to_all x1, waiting for transfers between devices, on_device(): lax.all_to_all(outgoing, 'node', split_axis=0, concat_axis=0, tiled=True)  140 us
    unnamed x15, waiting for transfers between devices  121 us
    reduce_scatter x1, waiting for transfers between devices, on_device(): lax.psum_scatter(term_edge_hidden.astype(jnp.bfloat16), 'node', scatter_d...  74.6 us
    reduce_scatter x1, waiting for transfers between devices, on_device(): lax.psum_scatter(term_edge_out.astype(jnp.bfloat16), 'node', scatter_dime...  73.8 us
    reduce_scatter x1, waiting for transfers between devices, on_device(): lax.psum_scatter(term_node_hidden.astype(jnp.bfloat16), 'node', scatter_d...  73.7 us
    unnamed x50, local copies, waits for them, and re-layouts  64 us
    reduce_scatter x1, waiting for transfers between devices, on_device(): lax.psum_scatter(term_node_out.astype(jnp.bfloat16), 'node', scatter_dime...  55.5 us
    all_gather x1, waiting for transfers between devices, on_device(): message_full = lax.all_gather(message_grad, 'chan', axis=1, tiled=True)  30.6 us
  transfers between devices with their start and end apart: 14, of which 12 were waited for; matrix products, arithmetic and copies ran while one was open for 11% of the time, Pallas kernels for 0%

commit v1 on v0

v1 whole, which is shorter than its diff:
```python
import functools

import jax
import jax.numpy as jnp
from jax import lax
from jax.experimental import pallas as pl
from jax.experimental.pallas import tpu as pltpu
from jax.sharding import PartitionSpec as P

BF = jnp.bfloat16
F32 = jnp.float32
LANE = 128
NC = 2


def mm(a, b):
    return jnp.dot(a, b, preferred_element_type=F32)


def mm_nt(a, b):
    return lax.dot_general(a, b, (((1,), (1,)), ((), ())), preferred_element_type=F32)


def mm_tn(a, b):
    return lax.dot_general(a, b, (((0,), (0,)), ((), ())), preferred_element_type=F32)


def one_hot(mask):
    return jnp.where(mask, 1.0, 0.0).astype(BF)


def lane_iota(rows):
    return lax.broadcasted_iota(jnp.int32, (rows, LANE), 1).astype(F32)


def sublane_iota(rows):
    return lax.broadcasted_iota(jnp.int32, (rows, LANE), 0).astype(F32)


def select_lanes(index, width):
    lanes = lane_iota(index.shape[0])
    return jnp.concatenate(
        [one_hot(index == lanes + float(b * LANE)) for b in range(width // LANE)], axis=1
    )


def wide(ref, lead=()):
    groups = ref.shape[len(lead)]
    return jnp.concatenate([ref[(*lead, g)] for g in range(groups)], axis=1)


def kernel(
    dims,
    lat, ea, src, dst, sb, weh, weo, wnh, wno, nct, ect,
    gl, ge, out_eh, out_eo, out_nh, out_no,
    ssem, rsem,
    ei, ni, cot, mg, hidden, hpre, npre,
    src_b, dst_b, q_b, dt, slt, pt, rsel,
    rq_out, rq_in, row_out, row_in, ret_out, ret_in,
    srcc, dstc, nsum, mgc,
    w_eh, w_nh, w_no, w_eo,
    g_eh, g_nh, g_no, g_eo,
    pb_m, rx_m, ch_m, pb_n, rx_n, ch_n, pb_e, rx_e, ch_e,
    *rs_bufs,
):
    NX, NY, NZ = dims
    NN = NY * NZ
    E, N = ea.shape[0], lat.shape[0]
    RE, RN = E // NX, N // NX
    L = NX * NC * LANE
    HC = NX * LANE
    PER = E // 2 // NN
    SLOT = PER // 2
    edge_scale = float(E * NN) ** (-0.5)
    node_scale = float(N * NN) ** (-0.5)

    n, k = lax.axis_index("node"), lax.axis_index("chan")
    x, c = k // NC, k % NC
    y, z = n // NZ, n % NZ

    def at_x(j):
        return (x + j) % NX

    def x_peer(j):
        return (n, at_x(j) * NC + c)

    def y_peer(j):
        return (((y + j) % NY) * NZ + z, k)

    def z_peer(j):
        return (y * NZ + (z + j) % NZ, k)

    def n_peer(j):
        return ((n + j) % NN, k)

    sib = (n, x * NC + 1 - c)

    pending = []
    used = [0]

    def rcopy(a, b, device):
        i = used[0]
        used[0] += 1
        copy = pltpu.make_async_remote_copy(
            src_ref=a, dst_ref=b, send_sem=ssem.at[i], recv_sem=rsem.at[i],
            device_id=device, device_id_type=pl.DeviceIdType.MESH,
        )
        copy.start()
        pending.append(copy)
        return copy

    def flush():
        while pending:
            pending.pop(0).wait_send()

    far_first = sorted(range(1, NX), key=lambda j: -min(j, NX - j))

    class ToRows:
        def __init__(self, put):
            self.put, self.near, self.far = put, [], []

        def send(self, j, chunk):
            if j:
                self.far.append((j, rcopy(chunk, self.put(x * NC + c), x_peer(j))))
            else:
                self.put(x * NC + c)[...] = chunk[...]
                self.near.append(rcopy(chunk, self.put(x * NC + c), sib))
            return self

        def send_all(self, chunk):
            for j in [*far_first, 0]:
                self.send(j, chunk(at_x(j)))
            return self

        def forward(self):
            for j, copy in self.far:
                copy.wait_recv()
                slot = self.put(at_x(NX - j) * NC + c)
                self.near.append(rcopy(slot, slot, sib))

        def wait(self):
            for copy in self.near:
                copy.wait_recv()

    class ToChan:
        def __init__(self, value, pb, rx, ch):
            self.pb, self.rx, self.ch, self.far = pb, rx, ch, []
            for g in range(NX * NC):
                pb[g // NC, g % NC] = value[:, g * LANE:(g + 1) * LANE].astype(BF)
            self.near = [
                (j, rcopy(pb.at[at_x(j), 1 - c], rx.at[at_x(j)], sib)) for j in [*far_first, 0]
            ]

        def forward(self):
            for j, copy in self.near:
                copy.wait_recv()
                xx = at_x(j)
                total = (self.rx[xx].astype(F32) + self.pb[xx, c].astype(F32)).astype(BF)
                if j:
                    self.rx[xx] = total
                    self.far.append(rcopy(self.rx.at[xx], self.ch.at[x], x_peer(j)))
                else:
                    self.ch[x] = total

        def wait(self):
            for copy in self.far:
                copy.wait_recv()

    class Gather:
        def __init__(self, w):
            self.w, self.half = w, w.shape[2] // 2

        def step1(self, own):
            w = self.w
            self.copies = [
                rcopy(own, w.at[y, z, :, pl.ds((NX - j) * LANE, LANE)], x_peer(j))
                for j in range(1, NX)
            ]

        def _recv(self):
            for copy in self.copies:
                copy.wait_recv()

        def step2(self):
            self._recv()
            w, h = self.w, self.half
            a = w.at[y, z, pl.ds(0, h), pl.ds(LANE, HC - LANE)]
            b = w.at[y, z, pl.ds(h, h), pl.ds(LANE, HC - LANE)]
            self.copies = [rcopy(a, a, z_peer(j)) for j in range(1, NZ)]
            self.copies += [rcopy(b, b, y_peer(j)) for j in range(1, NY)]

        def step3(self):
            self._recv()
            w, h = self.w, self.half
            a = w.at[y, :, pl.ds(0, h), pl.ds(LANE, HC - LANE)]
            b = w.at[:, z, pl.ds(h, h), pl.ds(LANE, HC - LANE)]
            self.copies = [rcopy(a, a, y_peer(j)) for j in range(1, NY)]
            self.copies += [rcopy(b, b, z_peer(j)) for j in range(1, NZ)]

        def wait(self):
            self._recv()

    class Scatter:
        def __init__(self, g, bufs):
            self.g = g
            self.ra, self.rb, self.sa, self.sbb, self.ra2, self.rb2, self.s2, self.r3 = bufs

        def step1(self):
            g, half = self.g, HC // 2
            self.a = [
                rcopy(g.at[:, (z + j) % NZ, :, pl.ds(0, half)], self.ra.at[j - 1], z_peer(j))
                for j in range(1, NZ)
            ]
            self.b = [
                rcopy(g.at[(y + j) % NY, :, :, pl.ds(half, half)], self.rb.at[j - 1], y_peer(j))
                for j in range(1, NY)
            ]

        def step2(self):
            g, half = self.g, HC // 2
            for copy in self.a:
                copy.wait_recv()
            for yy in range(NY):
                total = g[yy, z, :, 0:half].astype(F32)
                for j in range(1, NZ):
                    total = total + self.ra[j - 1, yy].astype(F32)
                self.sa[yy] = total.astype(BF)
            self.a = [
                rcopy(self.sa.at[(y + j) % NY], self.ra2.at[j - 1], y_peer(j))
                for j in range(1, NY)
            ]
            for copy in self.b:
                copy.wait_recv()
            for zz in range(NZ):
                total = g[y, zz, :, half:HC].astype(F32)
                for j in range(1, NY):
                    total = total + self.rb[j - 1, zz].astype(F32)
                self.sbb[zz] = total.astype(BF)
            self.b = [
                rcopy(self.sbb.at[(z + j) % NZ], self.rb2.at[j - 1], z_peer(j))
                for j in range(1, NZ)
            ]

        def step3(self):
            half = HC // 2
            for copy in self.a:
                copy.wait_recv()
            total = self.sa[y].astype(F32)
            for j in range(1, NY):
                total = total + self.ra2[j - 1].astype(F32)
            self.s2[:, 0:half] = total.astype(BF)
            for copy in self.b:
                copy.wait_recv()
            total = self.sbb[z].astype(F32)
            for j in range(1, NZ):
                total = total + self.rb2[j - 1].astype(F32)
            self.s2[:, half:HC] = total.astype(BF)
            self.x = [
                rcopy(self.s2.at[:, pl.ds(j * LANE, LANE)], self.r3.at[j - 1], x_peer(j))
                for j in range(1, NX)
            ]

        def finish(self):
            for copy in self.x:
                copy.wait_recv()
            total = self.s2[:, 0:LANE].astype(F32)
            for j in range(1, NX):
                total = total + self.r3[j - 1].astype(F32)
            return total

    barrier = pltpu.get_barrier_semaphore()
    partners = [x_peer(j) for j in range(1, NX)] + [sib] + [n_peer(j) for j in range(1, NN)]
    for device in partners:
        pl.semaphore_signal(barrier, inc=1, device_id=device, device_id_type=pl.DeviceIdType.MESH)
    pl.semaphore_wait(barrier, len(partners))

    ch_eh, ch_nh = weh.shape[0] // NN, wnh.shape[0] // NN
    gat_eh, gat_nh, gat_no, gat_eo = Gather(w_eh), Gather(w_nh), Gather(w_no), Gather(w_eo)
    gat_eh.step1(weh.at[pl.ds(n * ch_eh, ch_eh), :])
    rows_ea = ToRows(lambda g: ei.at[2, g]).send_all(lambda xx: ea.at[pl.ds(xx * RE, RE), :])

    srcf = src[...].astype(F32)
    dstf = dst[...].astype(F32)
    is_far = srcf >= float(N)
    slotf = jnp.where(is_far, jnp.floor((srcf - float(N)) * (1.0 / LANE)), -1.0)
    blocks = E // LANE
    for b in range(blocks):
        piece = slice(b * LANE, (b + 1) * LANE)
        src_b[piece, :] = jnp.broadcast_to(srcf[:, piece], (LANE, LANE)).T
        dst_b[piece, :] = jnp.broadcast_to(dstf[:, piece], (LANE, LANE)).T
    src_col = src_b[...]
    slot_col = jnp.where(
        src_col >= float(N), jnp.floor((src_col - float(N)) * (1.0 / LANE)), -1.0
    )
    order = sublane_iota(E)
    place = sublane_iota(NN * PER)
    for b in range(blocks):
        piece = slice(b * LANE, (b + 1) * LANE)
        mine = jnp.broadcast_to(slotf[:, piece], (E, LANE))
        before = (slot_col == mine) & (order < lane_iota(E) + float(b * LANE))
        rank = jnp.sum(jnp.where(before, 1.0, 0.0), axis=0, keepdims=True)
        q = jnp.where(is_far[:, piece], slotf[:, piece] * float(SLOT) + rank, -1.0)
        pt[:, piece] = one_hot(place == jnp.broadcast_to(q, (NN * PER, LANE)))
        q_b[piece, :] = jnp.broadcast_to(q, (LANE, LANE)).T
    row_in_block = (src_col - LANE * jnp.floor(src_col * (1.0 / LANE))).astype(BF)
    wanted = mm(pt[...], row_in_block).astype(BF)
    for p in range(NN):
        rq_out[p] = wanted[p * PER:(p + 1) * PER]
    ask = [
        rcopy(rq_out.at[(n + j) % NN], rq_in.at[n], n_peer(j)) for j in range(1, NN)
    ]
    rq_in[n] = rq_out[n]

    rows_dst = ToRows(lambda g: ei.at[1, g])
    for j in [*far_first, 0]:
        xx = at_x(j)
        pick = select_lanes(dst_b[pl.ds(xx * RE, RE), :], N)
        dstc[xx] = mm(pick, lat[...]).astype(BF)
        rows_dst.send(j, dstc.at[xx])

    gat_eh.step2()

    w_eh[:, :, :, 0:LANE] = weh[...].reshape(NY, NZ, ch_eh, LANE)
    w_nh[:, :, :, 0:LANE] = wnh[...].reshape(NY, NZ, ch_nh, LANE)
    w_eo[:, :, :, 0:LANE] = weo[...].T.reshape(NY, NZ, L // NN, LANE)
    w_no[:, :, :, 0:LANE] = wno[...].T.reshape(NY, NZ, L // NN, LANE)
    for gather in (gat_eo, gat_nh, gat_no):
        gather.step1(gather.w.at[y, z, :, pl.ds(0, LANE)])

    for copy in ask:
        copy.wait_recv()
    half_rows = sublane_iota(PER) < float(SLOT)
    for d in range(NN):
        base = jnp.where(
            half_rows,
            (sb[0, d, 0] * LANE).astype(F32),
            (sb[0, d, 1] * LANE).astype(F32),
        )
        rsel[d] = select_lanes(rq_in[d].astype(F32) + base, N)
    given = mm(rsel[...].reshape(NN * PER, N), lat[...]).astype(BF)
    for d in range(NN):
        row_out[d] = given[d * PER:(d + 1) * PER]
    halo = [
        rcopy(row_out.at[(n + j) % NN], row_in.at[n], n_peer(j)) for j in range(1, NN)
    ]
    row_in[n] = row_out[n]

    gat_eh.step3()
    rows_ea.forward()
    rows_dst.forward()

    nodes_down = sublane_iota(N)
    for b in range(blocks):
        piece = slice(b * LANE, (b + 1) * LANE)
        dt[:, piece] = one_hot(nodes_down == jnp.broadcast_to(dstf[:, piece], (N, LANE)))
        slt[:, piece] = one_hot(nodes_down == jnp.broadcast_to(srcf[:, piece], (N, LANE)))

    for copy in halo:
        copy.wait_recv()
    table = jnp.concatenate([lat[...], row_in[...].reshape(NN * PER, LANE)], axis=0)
    rows_src = ToRows(lambda g: ei.at[0, g])
    for j in [*far_first, 0]:
        xx = at_x(j)
        here = pl.ds(xx * RE, RE)
        pick = jnp.concatenate(
            [select_lanes(src_b[here, :], N), select_lanes(q_b[here, :], NN * PER)], axis=1
        )
        srcc[xx] = mm(pick, table).astype(BF)
        rows_src.send(j, srcc.at[xx])
    rows_lat = ToRows(lambda g: ni.at[0, g]).send_all(lambda xx: lat.at[pl.ds(xx * RN, RN), :])
    rows_cot = ToRows(lambda g: cot.at[g]).send_all(lambda xx: nct.at[pl.ds(xx * RN, RN), :])
    for gather in (gat_eo, gat_nh, gat_no):
        gather.step2()

    gat_eh.wait()
    rows_ea.wait()
    rows_dst.wait()
    weh_all = w_eh[...].reshape(3 * L, HC)
    hpre[...] = mm(wide(ei, (1,)), weh_all[L:2 * L]) + mm(wide(ei, (2,)), weh_all[2 * L:])
    gat_eo.step3()
    rows_src.forward()
    rows_src.wait()
    pre = hpre[...] + mm(wide(ei, (0,)), weh_all[:L])
    hpre[...] = pre
    hidden[...] = (pre * jax.nn.sigmoid(pre)).astype(BF)
    gat_eo.wait()
    weo_all = w_eo[...].reshape(L, HC)
    chan_m = ToChan(mm_nt(hidden[...], weo_all), pb_m, rx_m, ch_m)
    gat_nh.step3()
    gat_no.step3()
    chan_m.forward()
    rows_lat.forward()
    rows_cot.forward()
    chan_m.wait()

    fresh = (ea[...].astype(F32) + ch_m[...].reshape(E, LANE).astype(F32)).astype(BF)
    nsum[...] = mm(dt[...], fresh).astype(BF).reshape(NX, RN, LANE)
    rows_sum = ToRows(lambda g: ni.at[1, g]).send_all(lambda xx: nsum.at[xx])

    rows_lat.wait()
    rows_cot.wait()
    gat_nh.wait()
    gat_no.wait()
    wnh_all = w_nh[...].reshape(2 * L, HC)
    cots = wide(cot)
    npre[...] = mm(wide(ni, (0,)), wnh_all[:L])
    pulled = mm(cots, w_no[...].reshape(L, HC))
    rows_sum.forward()
    rows_sum.wait()
    pre = npre[...] + mm(wide(ni, (1,)), wnh_all[L:])
    sig = jax.nn.sigmoid(pre)
    node_hidden = (pre * sig).astype(BF)
    node_back = (pulled * (sig * (1.0 + pre * (1.0 - sig)))).astype(BF)
    chan_n1 = ToChan(mm_nt(node_back, wnh_all[L:]), pb_n.at[1], rx_n.at[1], ch_n.at[1])
    chan_n0 = ToChan(mm_nt(node_back, wnh_all[:L]), pb_n.at[0], rx_n.at[0], ch_n.at[0])
    chan_n1.forward()
    chan_n0.forward()

    def weight_grad(g, values, back):
        per_y = g.shape[1] * g.shape[2]
        for yy in range(NY):
            part = mm_tn(values[:, yy * per_y:(yy + 1) * per_y], back)
            g[yy] = part.astype(BF).reshape(g.shape[1:])

    sc = [Scatter(g, rs_bufs[8 * i:8 * i + 8]) for i, g in enumerate((g_eh, g_nh, g_no, g_eo))]
    sc_eh, sc_nh, sc_no, sc_eo = sc
    weight_grad(g_nh, jnp.concatenate([wide(ni, (0,)), wide(ni, (1,))], axis=1), node_back)
    sc_nh.step1()
    weight_grad(g_no, cots, node_hidden)
    sc_no.step1()

    chan_n1.wait()
    share = ch_n[1].reshape(N, LANE)
    rows_mg = ToRows(lambda g: mg.at[g])
    for j in [*far_first, 0]:
        xx = at_x(j)
        here = pl.ds(xx * RE, RE)
        total = ect[here, :].astype(F32) + mm(select_lanes(dst_b[here, :], N), share)
        ge[here, :] = total
        mgc[xx] = total.astype(BF)
        rows_mg.send(j, mgc.at[xx])
    pre = hpre[...]
    sig = jax.nn.sigmoid(pre)
    hpre[...] = sig * (1.0 + pre * (1.0 - sig))
    rows_mg.forward()
    rows_mg.wait()
    message_grad = wide(mg)
    edge_back = (mm(message_grad, weo_all) * hpre[...]).astype(BF)
    chan_e = [
        ToChan(
            mm_nt(edge_back, weh_all[t * L:(t + 1) * L]), pb_e.at[t], rx_e.at[t], ch_e.at[t]
        )
        for t in range(3)
    ]
    chan_e[0].forward()
    weight_grad(
        g_eh, jnp.concatenate([wide(ei, (t,)) for t in range(3)], axis=1), edge_back
    )
    sc_eh.step1()
    chan_e[1].forward()
    weight_grad(g_eo, message_grad, hidden[...])
    sc_eo.step1()
    chan_e[2].forward()
    sc_nh.step2()
    sc_no.step2()

    chan_e[0].wait()
    from_source = ch_e[0].reshape(E, LANE)
    back = mm(pt[...], from_source).astype(BF)
    for p in range(NN):
        ret_out[p] = back[p * PER:(p + 1) * PER]
    returned = [
        rcopy(ret_out.at[(n + j) % NN], ret_in.at[n], n_peer(j)) for j in range(1, NN)
    ]
    ret_in[n] = ret_out[n]
    sc_nh.step3()
    sc_no.step3()
    chan_n0.wait()
    chan_e[1].wait()
    gl[...] = (
        nct[...].astype(F32)
        + ch_n[0].reshape(N, LANE).astype(F32)
        + mm(slt[...], from_source)
        + mm(dt[...], ch_e[1].reshape(E, LANE))
    )
    sc_eh.step2()
    sc_eo.step2()
    chan_e[2].wait()
    ge[...] = ge[...] + ch_e[2].reshape(E, LANE).astype(F32)
    for copy in returned:
        copy.wait_recv()
    gl[...] = gl[...] + mm_tn(
        rsel[...].reshape(NN * PER, N), ret_in[...].reshape(NN * PER, LANE)
    )
    sc_eh.step3()
    sc_eo.step3()
    out_nh[...] = node_scale * sc_nh.finish()
    out_no[...] = (node_scale * sc_no.finish()).T
    out_eh[...] = edge_scale * sc_eh.finish()
    out_eo[...] = (edge_scale * sc_eo.finish()).T
    flush()


def on_device(
    dims,
    latents, edge_attr, edge_src, edge_dst, send_blocks,
    edge_hidden_w, edge_out_w, node_hidden_w, node_out_w,
    node_cotangent, edge_cotangent,
):
    NX, NY, NZ = dims
    NN = NY * NZ
    E, N = edge_attr.shape[0], latents.shape[0]
    RE, RN = E // NX, N // NX
    G = NX * NC
    L, HC = G * LANE, NX * LANE
    PER = E // 2 // NN

    def v(*shape, dtype=BF):
        return pltpu.VMEM(shape, dtype)

    chunks = [3 * L // NN, 2 * L // NN, L // NN, L // NN]
    rs = []
    for ch in chunks:
        rs += [
            v(NZ - 1, NY, ch, HC // 2), v(NY - 1, NZ, ch, HC // 2),
            v(NY, ch, HC // 2), v(NZ, ch, HC // 2),
            v(NY - 1, ch, HC // 2), v(NZ - 1, ch, HC // 2),
            v(ch, HC), v(NX - 1, ch, LANE),
        ]
    scratch = [
        pltpu.SemaphoreType.DMA((320,)), pltpu.SemaphoreType.DMA((320,)),
        v(3, G, RE, LANE), v(2, G, RN, LANE), v(G, RN, LANE), v(G, RE, LANE),
        v(RE, HC), v(RE, HC, dtype=F32), v(RN, HC, dtype=F32),
        v(E, LANE, dtype=F32), v(E, LANE, dtype=F32), v(E, LANE, dtype=F32),
        v(N, E), v(N, E), v(NN * PER, E), v(NN, PER, N),
        *[v(NN, PER, LANE) for _ in range(6)],
        v(NX, RE, LANE), v(NX, RE, LANE), v(NX, RN, LANE), v(NX, RE, LANE),
        *[v(NY, NZ, ch, HC) for ch in chunks],
        *[v(NY, NZ, ch, HC) for ch in chunks],
        v(NX, NC, RE, LANE), v(NX, RE, LANE), v(NX, RE, LANE),
        v(2, NX, NC, RN, LANE), v(2, NX, RN, LANE), v(2, NX, RN, LANE),
        v(3, NX, NC, RE, LANE), v(3, NX, RE, LANE), v(3, NX, RE, LANE),
        *rs,
    ]
    vmem = pl.BlockSpec(memory_space=pltpu.VMEM)
    smem = pl.BlockSpec(memory_space=pltpu.SMEM)

    def f(*shape):
        return jax.ShapeDtypeStruct(shape, F32)

    return pl.pallas_call(
        functools.partial(kernel, dims),
        out_shape=(
            f(N, LANE), f(E, LANE), f(chunks[0], LANE), f(LANE, chunks[3]),
            f(chunks[1], LANE), f(LANE, chunks[2]),
        ),
        in_specs=[vmem] * 4 + [smem] + [vmem] * 6,
        out_specs=[vmem] * 6,
        scratch_shapes=scratch,
        compiler_params=pltpu.CompilerParams(
            collective_id=0, has_side_effects=True, vmem_limit_bytes=64 * 1024 * 1024 - 65536
        ),
    )(
        latents, edge_attr, edge_src.reshape(1, E), edge_dst.reshape(1, E), send_blocks,
        edge_hidden_w, edge_out_w, node_hidden_w, node_out_w, node_cotangent, edge_cotangent,
    )


def solution(mesh):
    nodes, chans = mesh.shape["node"], mesh.shape["chan"]
    nz = 1
    while nz * nz < nodes:
        nz *= 2
    dims = (chans // NC, nodes // nz, nz)
    return jax.shard_map(
        functools.partial(on_device, dims),
        mesh=mesh,
        in_specs=(
            P("node", "chan"),
            P("node", "chan"),
            P("node"),
            P("node"),
            P("node", None, None),
            P(None, "chan"),
            P("chan", None),
            P(None, "chan"),
            P("chan", None),
            P("node", "chan"),
            P("node", "chan"),
        ),
        out_specs=(
            P("node", "chan"),
            P("node", "chan"),
            P("node", "chan"),
            P("chan", "node"),
            P("node", "chan"),
            P("chan", "node"),
        ),
        check_vma=False,
    )
```

time: 887 us -> 145 us (0.16)
  waiting for transfers between devices: 642 us -> 0 us
  Pallas kernels: 0 us -> 134 us
  local copies, waits for them, and re-layouts: 120 us -> 10 us
  other arithmetic: 53.7 us -> 0 us
  matrix products: 40.1 us -> 0 us
  starting transfers between devices: 15 us -> 0 us
  between operations: 14.5 us -> 0.66 us
    reduce_scatter x4 -> x0, waiting for transfers between devices: 278 us -> none  [the longest x1 74.6 us: on_device(): lax.psum_scatter(term_edge_hidden.astype(jnp.bfloat16), 'node', scatter_d...]
    all_to_all x2 -> x0, waiting for transfers between devices: 140 us -> none  [the longest x1 140 us: on_device(): lax.all_to_all(outgoing, 'node', split_axis=0, concat_axis=0, tiled=True)]
    pallas_call x0 -> x1, Pallas kernels: none -> 134 us  [on_device(): pl.pallas_call(functools.partial(kernel, dims), out_shape=(f(N, LANE), f(...]
    unnamed x15 -> x0, waiting for transfers between devices: 121 us -> none
    all_gather x5 -> x0, waiting for transfers between devices: 103 us -> none  [the longest x1 30.6 us: on_device(): message_full = lax.all_gather(message_grad, 'chan', axis=1, tiled=True)]
    unnamed x50 -> x15, local copies, waits for them, and re-layouts: 64 us -> 4.99 us
    dot_general x11 -> x0, matrix products: 40.1 us -> none  [the longest x1 7.26 us: on_device(): jnp.dot(edge_inputs.T, edge_hidden_grad, preferred_element_type=jnp.float32)]
    scatter-add x4 -> x0, other arithmetic: 31.1 us -> none  [the longest x1 10.4 us: on_device(): jax.ops.segment_sum(edge_input_grad[:, 0], edge_src, num_segments=table_s...]
  transfers between devices with their start and end apart: 14 -> 0, of which waited for: 12 -> 0; matrix products, arithmetic and copies ran while one was open for 11% -> 0% of each run, Pallas kernels for 0% -> 0%
where the time goes in v1:
time: 145 us
  Pallas kernels  134 us (92%)
  local copies, waits for them, and re-layouts  10 us (7%)
    pallas_call x1, Pallas kernels, on_device(): pl.pallas_call(functools.partial(kernel, dims), out_shape=(f(N, LANE), f(...  134 us
    unnamed x15, local copies, waits for them, and re-layouts  4.99 us
    pallas_call x2, local copies, waits for them, and re-layouts, on_device(): pl.pallas_call(functools.partial(kernel, dims), out_shape=(f(N, LANE), f(...  3.15 us

profile of v1, /device:TPU:0, one launch (start us, length us, event | category | flops | bytes accessed | tf_op | source)
XLA Modules:
  0.0 144.5 jit_solution(662004194486444323)
XLA Ops:
  0.6 0.0 copy-start.3
  0.6 1.3 reshape.18.src
  1.9 0.0 copy-done.3
  1.9 0.0 copy-start.4
  1.9 0.6 reshape.19.dst
  2.5 0.1 copy-done.4
  2.6 0.7 copy.17.sb
  3.3 133.8 %shard_map.154 = (f32[768,128]{1,0:T(8,128)}, f32[1536,128]{1,0:T(8,128)}, f32[192,128]{1,0:T(8,128)}, f32[128,64]{1,0:T(8,128)}, f32[128,128]{1,0:T(8,128)}, /*index=5*/f32[128,64]{1,0:T(8,128)}) custom-call(bf16[768,128]{1,0:T(8,128)(2,1)} %lat.1, bf16[1536,128]{1,0:T(8,128)(2,1)} %ea.1, s32[1,1536]{1,0:T(1,128)} %reshape.18.src, s32[1,1536]{1,0:T(1,128)} %reshape.19.dst, ...), custom_call_target="tpu_custom_call" | custom-call | tf_op jit(solution)/shard_map/pallas_call | solution.py:551
  137.1 0.0 copy-start
  137.1 1.6 %copy.18 = f32[128,64]{0,1:T(8,128)} copy(f32[128,64]{1,0:T(8,128)} %get-tuple-element.9) | data formatting | bytes 65536 | tf_op jit(solution)/shard_map/pallas_call | solution.py:551
  138.7 1.5 %copy.19 = f32[128,64]{0,1:T(8,128)} copy(f32[128,64]{1,0:T(8,128)} %get-tuple-element.11) | data formatting | bytes 65536 | tf_op jit(solution)/shard_map/pallas_call | solution.py:551
  140.3 1.8 %copy.24 = f32[768,128]{1,0:T(8,128)} copy(f32[768,128]{1,0:T(8,128)} %get-tuple-element.18) | data formatting | bytes 786432
  142.0 0.0 copy-done
  142.0 0.0 copy-start.1
  142.1 0.9 copy.25
  142.9 0.1 copy-done.1
  143.0 0.0 copy-start.2
  143.0 0.6 copy.26
  143.7 0.2 copy-done.2
  143.9 0.6 copy.27
Async XLA Ops:
  0.6 1.3 copy-start.3
  1.9 0.7 copy-start.4
  137.1 4.9 %copy-start = (f32[1536,128]{1,0:T(8,128)S(1)}, f32[1536,128]{1,0:T(8,128)}, u32[]{:S(2)}) copy-start(f32[1536,128]{1,0:T(8,128)} %get-tuple-element.19) | copy-start | bytes 2359300
  142.0 1.0 copy-start.1
  143.0 0.9 copy-start.2

commit v2 on v1

--- a/solution.py
+++ b/solution.py
@@ -51,9 +51,10 @@
 
 def kernel(
     dims,
-    lat, ea, src, dst, sb, weh, weo, wnh, wno, nct, ect,
-    gl, ge, out_eh, out_eo, out_nh, out_no,
-    ssem, rsem,
+    lat_hbm, ea_hbm, src, dst, sb, weh, weo_hbm, wnh, wno_hbm, nct_hbm, ect_hbm,
+    gl_hbm, ge_hbm, out_eh, out_eo, out_nh, out_no,
+    ssem, rsem, lsem,
+    lat, ea, weo, wno, nct, ect, gl, ge,
     ei, ni, cot, mg, hidden, hpre, npre,
     src_b, dst_b, q_b, dt, slt, pt, rsel,
     rq_out, rq_in, row_out, row_in, ret_out, ret_in,
@@ -192,54 +193,154 @@
         def step3(self):
             self._recv()
             w, h = self.w, self.half
-            a = w.at[y, :, pl.ds(0, h), pl.ds(LANE, HC - LANE)]
-            b = w.at[:, z, pl.ds(h, h), pl.ds(LANE, HC - LANE)]
-            self.copies = [rcopy(a, a, y_peer(j)) for j in range(1, NY)]
-            self.copies += [rcopy(b, b, z_peer(j)) for j in range(1, NZ)]
+            rest = pl.ds(LANE, HC - LANE)
+            self.rings = [
+                (lambda yy, part: w.at[yy, part, pl.ds(0, h), rest], y, NY, y_peer, NZ),
+                (lambda zz, part: w.at[part, zz, pl.ds(h, h), rest], z, NZ, z_peer, NY),
+            ]
+            self.copies = []
+            for place, me, size, peer, across in self.rings:
+                mine = place(me, pl.ds(0, across))
+                self.copies.append([
+                    rcopy(mine, mine, peer(j)) for j in sorted({1, size - 1})
+                ])
+
+        def step4(self):
+            sent, self.copies = self.copies, []
+            for (place, me, size, peer, across), ring in zip(self.rings, sent):
+                if size == 2:
+                    self.copies += ring
+                    continue
+                part = across // 2
+                for copy, j, first in ((ring[0], 1, 0), (ring[1], size - 1, part)):
+                    copy.wait_recv()
+                    passed = place((me + size - j) % size, pl.ds(first, part))
+                    self.copies.append(rcopy(passed, passed, peer(j)))
 
         def wait(self):
             self._recv()
 
     class Scatter:
-        def __init__(self, g, bufs):
+        def __init__(self, g, bufs, over_x=False):
             self.g = g
-            self.ra, self.rb, self.sa, self.sbb, self.ra2, self.rb2, self.s2, self.r3 = bufs
+            self.ra, self.rb, self.sa, self.sbb, self.ra2, self.rb2, self.s2, self.r3 = bufs[:8]
+            self.main = self.s2.shape[0]
+            self.over_x = over_x
+            if over_x:
+                self.rx1, self.sx, self.rx2, self.sx2, self.rx3 = bufs[8:]
+            half, rows = HC // 2, pl.ds(0, self.main)
+            self.rings = (
+                (lambda d, part: (part, (z + d) % NZ, rows, pl.ds(0, half)),
+                 self.ra, NZ, z_peer, NY),
+                (lambda d, part: ((y + d) % NY, part, rows, pl.ds(half, half)),
+                 self.rb, NY, y_peer, NZ),
+            )
 
         def step1(self):
-            g, half = self.g, HC // 2
-            self.a = [
-                rcopy(g.at[:, (z + j) % NZ, :, pl.ds(0, half)], self.ra.at[j - 1], z_peer(j))
-                for j in range(1, NZ)
-            ]
-            self.b = [
-                rcopy(g.at[(y + j) % NY, :, :, pl.ds(half, half)], self.rb.at[j - 1], y_peer(j))
-                for j in range(1, NY)
-            ]
+            self.relay, self.full = [], []
+            for index, land, size, peer, across in self.rings:
+                part = across // 2
+                lo, hi = pl.ds(0, part), pl.ds(part, part)
+                if size == 2:
+                    continue
+                self.relay.append([
+                    rcopy(self.g.at[index(2, lo)], land.at[1, lo], peer(1)),
+                    rcopy(self.g.at[index(2, hi)], land.at[1, hi], peer(3)),
+                ])
+
+        def step1b(self):
+            for index, land, size, peer, across in self.rings:
+                part = across // 2
+                lo, hi = pl.ds(0, part), pl.ds(part, part)
+                if size == 2:
+                    every = pl.ds(0, across)
+                    self.full.append([rcopy(self.g.at[index(1, every)], land.at[0], peer(1))])
+                else:
+                    self.full.append([
+                        rcopy(self.g.at[index(1, hi)], land.at[0, hi], peer(1)),
+                        rcopy(self.g.at[index(3, lo)], land.at[2, lo], peer(3)),
+                    ])
+            if self.over_x:
+                part = pl.ds(self.main, self.g.shape[2] - self.main)
+                self.xs = [
+                    rcopy(
+                        self.g.at[:, :, part, pl.ds(j * LANE, LANE)], self.rx1.at[j - 1], x_peer(j)
+                    )
+                    for j in range(1, NX)
+                ]
+
+        def step1c(self):
+            for (index, land, size, peer, across), relay, full in zip(
+                self.rings, self.relay, self.full
+            ):
+                part = across // 2
+                for copy, j, here in (
+                    (relay[0], 1, pl.ds(0, part)), (relay[1], 3, pl.ds(part, part))
+                ):
+                    copy.wait_recv()
+                    at = index(j, here)
+                    self.g[at] = (
+                        self.g[at].astype(F32) + land[1, here].astype(F32)
+                    ).astype(BF)
+                    full.append(rcopy(self.g.at[at], land.at[j - 1, here], peer(j)))
 
         def step2(self):
-            g, half = self.g, HC // 2
-            for copy in self.a:
+            g, half, m = self.g, HC // 2, self.main
+            for copy in self.full[0]:
                 copy.wait_recv()
             for yy in range(NY):
-                total = g[yy, z, :, 0:half].astype(F32)
-                for j in range(1, NZ):
+                total = g[yy, z, 0:m, 0:half].astype(F32)
+                for j in sorted({1, NZ - 1}):
                     total = total + self.ra[j - 1, yy].astype(F32)
                 self.sa[yy] = total.astype(BF)
             self.a = [
                 rcopy(self.sa.at[(y + j) % NY], self.ra2.at[j - 1], y_peer(j))
                 for j in range(1, NY)
             ]
-            for copy in self.b:
+            for copy in self.full[1]:
                 copy.wait_recv()
             for zz in range(NZ):
-                total = g[y, zz, :, half:HC].astype(F32)
-                for j in range(1, NY):
+                total = g[y, zz, 0:m, half:HC].astype(F32)
+                for j in sorted({1, NY - 1}):
                     total = total + self.rb[j - 1, zz].astype(F32)
                 self.sbb[zz] = total.astype(BF)
             self.b = [
                 rcopy(self.sbb.at[(z + j) % NZ], self.rb2.at[j - 1], z_peer(j))
                 for j in range(1, NZ)
             ]
+
+        def x_step2(self):
+            for copy in self.xs:
+                copy.wait_recv()
+            for yy in range(NY):
+                total = self.g[yy, :, self.main:, 0:LANE].astype(F32)
+                for j in range(1, NX):
+                    total = total + self.rx1[j - 1, yy].astype(F32)
+                self.sx[yy] = total.astype(BF)
+            self.xs = [
+                rcopy(self.sx.at[:, (z + j) % NZ], self.rx2.at[j - 1], z_peer(j))
+                for j in range(1, NZ)
+            ]
+
+        def x_step3(self):
+            for copy in self.xs:
+                copy.wait_recv()
+            total = self.sx[:, z].astype(F32)
+            for j in range(1, NZ):
+                total = total + self.rx2[j - 1].astype(F32)
+            self.sx2[...] = total.astype(BF)
+            self.xs = [
+                rcopy(self.sx2.at[(y + j) % NY], self.rx3.at[j - 1], y_peer(j))
+                for j in range(1, NY)
+            ]
+
+        def x_finish(self):
+            for copy in self.xs:
+                copy.wait_recv()
+            total = self.sx2[y].astype(F32)
+            for j in range(1, NY):
+                total = total + self.rx3[j - 1].astype(F32)
+            return total
 
         def step3(self):
             half = HC // 2
@@ -268,19 +369,26 @@
                 total = total + self.r3[j - 1].astype(F32)
             return total
 
+    def local(a, b, i):
+        copy = pltpu.make_async_copy(a, b, lsem.at[i])
+        copy.start()
+        return copy
+
     barrier = pltpu.get_barrier_semaphore()
     partners = [x_peer(j) for j in range(1, NX)] + [sib] + [n_peer(j) for j in range(1, NN)]
     for device in partners:
         pl.semaphore_signal(barrier, inc=1, device_id=device, device_id_type=pl.DeviceIdType.MESH)
-    pl.semaphore_wait(barrier, len(partners))
-
-    ch_eh, ch_nh = weh.shape[0] // NN, wnh.shape[0] // NN
-    gat_eh, gat_nh, gat_no, gat_eo = Gather(w_eh), Gather(w_nh), Gather(w_no), Gather(w_eo)
-    gat_eh.step1(weh.at[pl.ds(n * ch_eh, ch_eh), :])
-    rows_ea = ToRows(lambda g: ei.at[2, g]).send_all(lambda xx: ea.at[pl.ds(xx * RE, RE), :])
-
-    srcf = src[...].astype(F32)
-    dstf = dst[...].astype(F32)
+    get_lat, get_weo, get_wno, get_weh, get_wnh, get_ea, get_nct, get_ect = [
+        local(a, b, i)
+        for i, (a, b) in enumerate((
+            (lat_hbm, lat), (weo_hbm, weo), (wno_hbm, wno),
+            (weh, w_eh.at[:, :, :, pl.ds(0, LANE)]), (wnh, w_nh.at[:, :, :, pl.ds(0, LANE)]),
+            (ea_hbm, ea), (nct_hbm, nct), (ect_hbm, ect),
+        ))
+    ]
+
+    srcf = src[...].reshape(1, E).astype(F32)
+    dstf = dst[...].reshape(1, E).astype(F32)
     is_far = srcf >= float(N)
     slotf = jnp.where(is_far, jnp.floor((srcf - float(N)) * (1.0 / LANE)), -1.0)
     blocks = E // LANE
@@ -306,10 +414,24 @@
     wanted = mm(pt[...], row_in_block).astype(BF)
     for p in range(NN):
         rq_out[p] = wanted[p * PER:(p + 1) * PER]
+    get_weo.wait()
+    get_wno.wait()
+    w_eo[:, :, :, 0:LANE] = weo[...].T.reshape(NY, NZ, L // NN, LANE)
+    w_no[:, :, :, 0:LANE] = wno[...].T.reshape(NY, NZ, L // NN, LANE)
+    pl.semaphore_wait(barrier, len(partners))
+
+    gat_eh, gat_nh, gat_no, gat_eo = Gather(w_eh), Gather(w_nh), Gather(w_no), Gather(w_eo)
+    gat_eh.step1(weh.at[y, z])
     ask = [
         rcopy(rq_out.at[(n + j) % NN], rq_in.at[n], n_peer(j)) for j in range(1, NN)
     ]
     rq_in[n] = rq_out[n]
+    get_lat.wait()
+    get_ea.wait()
+    rows_ea = ToRows(lambda g: ei.at[2, g]).send_all(lambda xx: ea.at[pl.ds(xx * RE, RE), :])
+    gat_eo.step1(w_eo.at[y, z, :, pl.ds(0, LANE)])
+    gat_nh.step1(wnh.at[y, z])
+    gat_no.step1(w_no.at[y, z, :, pl.ds(0, LANE)])
 
     rows_dst = ToRows(lambda g: ei.at[1, g])
     for j in [*far_first, 0]:
@@ -320,21 +442,14 @@
 
     gat_eh.step2()
 
-    w_eh[:, :, :, 0:LANE] = weh[...].reshape(NY, NZ, ch_eh, LANE)
-    w_nh[:, :, :, 0:LANE] = wnh[...].reshape(NY, NZ, ch_nh, LANE)
-    w_eo[:, :, :, 0:LANE] = weo[...].T.reshape(NY, NZ, L // NN, LANE)
-    w_no[:, :, :, 0:LANE] = wno[...].T.reshape(NY, NZ, L // NN, LANE)
-    for gather in (gat_eo, gat_nh, gat_no):
-        gather.step1(gather.w.at[y, z, :, pl.ds(0, LANE)])
-
     for copy in ask:
         copy.wait_recv()
     half_rows = sublane_iota(PER) < float(SLOT)
     for d in range(NN):
         base = jnp.where(
             half_rows,
-            (sb[0, d, 0] * LANE).astype(F32),
-            (sb[0, d, 1] * LANE).astype(F32),
+            (sb[0, d] * LANE).astype(F32),
+            (sb[1, d] * LANE).astype(F32),
         )
         rsel[d] = select_lanes(rq_in[d].astype(F32) + base, N)
     given = mm(rsel[...].reshape(NN * PER, N), lat[...]).astype(BF)
@@ -345,15 +460,21 @@
     ]
     row_in[n] = row_out[n]
 
+    gat_eo.step2()
     gat_eh.step3()
     rows_ea.forward()
     rows_dst.forward()
+    gat_nh.step2()
+    gat_no.step2()
 
     nodes_down = sublane_iota(N)
     for b in range(blocks):
         piece = slice(b * LANE, (b + 1) * LANE)
         dt[:, piece] = one_hot(nodes_down == jnp.broadcast_to(dstf[:, piece], (N, LANE)))
         slt[:, piece] = one_hot(nodes_down == jnp.broadcast_to(srcf[:, piece], (N, LANE)))
+
+    gat_eo.step3()
+    gat_eh.step4()
 
     for copy in halo:
         copy.wait_recv()
@@ -367,18 +488,22 @@
         )
         srcc[xx] = mm(pick, table).astype(BF)
         rows_src.send(j, srcc.at[xx])
-    rows_lat = ToRows(lambda g: ni.at[0, g]).send_all(lambda xx: lat.at[pl.ds(xx * RN, RN), :])
-    rows_cot = ToRows(lambda g: cot.at[g]).send_all(lambda xx: nct.at[pl.ds(xx * RN, RN), :])
-    for gather in (gat_eo, gat_nh, gat_no):
-        gather.step2()
-
+    gat_nh.step3()
+    gat_no.step3()
+    gat_eo.step4()
+
+    get_weh.wait()
     gat_eh.wait()
     rows_ea.wait()
     rows_dst.wait()
     weh_all = w_eh[...].reshape(3 * L, HC)
     hpre[...] = mm(wide(ei, (1,)), weh_all[L:2 * L]) + mm(wide(ei, (2,)), weh_all[2 * L:])
-    gat_eo.step3()
     rows_src.forward()
+    get_nct.wait()
+    rows_lat = ToRows(lambda g: ni.at[0, g]).send_all(lambda xx: lat.at[pl.ds(xx * RN, RN), :])
+    rows_cot = ToRows(lambda g: cot.at[g]).send_all(lambda xx: nct.at[pl.ds(xx * RN, RN), :])
+    gat_nh.step4()
+    gat_no.step4()
     rows_src.wait()
     pre = hpre[...] + mm(wide(ei, (0,)), weh_all[:L])
     hpre[...] = pre
@@ -386,8 +511,6 @@
     gat_eo.wait()
     weo_all = w_eo[...].reshape(L, HC)
     chan_m = ToChan(mm_nt(hidden[...], weo_all), pb_m, rx_m, ch_m)
-    gat_nh.step3()
-    gat_no.step3()
     chan_m.forward()
     rows_lat.forward()
     rows_cot.forward()
@@ -399,6 +522,7 @@
 
     rows_lat.wait()
     rows_cot.wait()
+    get_wnh.wait()
     gat_nh.wait()
     gat_no.wait()
     wnh_all = w_nh[...].reshape(2 * L, HC)
@@ -422,15 +546,18 @@
             part = mm_tn(values[:, yy * per_y:(yy + 1) * per_y], back)
             g[yy] = part.astype(BF).reshape(g.shape[1:])
 
-    sc = [Scatter(g, rs_bufs[8 * i:8 * i + 8]) for i, g in enumerate((g_eh, g_nh, g_no, g_eo))]
-    sc_eh, sc_nh, sc_no, sc_eo = sc
+    sc_eh, sc_eo = Scatter(g_eh, rs_bufs[0:13], True), Scatter(g_eo, rs_bufs[13:26], True)
+    sc_nh, sc_no = Scatter(g_nh, rs_bufs[26:34]), Scatter(g_no, rs_bufs[34:42])
     weight_grad(g_nh, jnp.concatenate([wide(ni, (0,)), wide(ni, (1,))], axis=1), node_back)
     sc_nh.step1()
     weight_grad(g_no, cots, node_hidden)
     sc_no.step1()
+    sc_nh.step1b()
+    sc_no.step1b()
 
     chan_n1.wait()
     share = ch_n[1].reshape(N, LANE)
+    get_ect.wait()
     rows_mg = ToRows(lambda g: mg.at[g])
     for j in [*far_first, 0]:
         xx = at_x(j)
@@ -443,6 +570,8 @@
     sig = jax.nn.sigmoid(pre)
     hpre[...] = sig * (1.0 + pre * (1.0 - sig))
     rows_mg.forward()
+    sc_nh.step1c()
+    sc_no.step1c()
     rows_mg.wait()
     message_grad = wide(mg)
     edge_back = (mm(message_grad, weo_all) * hpre[...]).astype(BF)
@@ -460,9 +589,11 @@
     chan_e[1].forward()
     weight_grad(g_eo, message_grad, hidden[...])
     sc_eo.step1()
-    chan_e[2].forward()
     sc_nh.step2()
     sc_no.step2()
+    chan_e[2].forward()
+    sc_eh.step1b()
+    sc_eo.step1b()
 
     chan_e[0].wait()
     from_source = ch_e[0].reshape(E, LANE)
@@ -473,6 +604,8 @@
         rcopy(ret_out.at[(n + j) % NN], ret_in.at[n], n_peer(j)) for j in range(1, NN)
     ]
     ret_in[n] = ret_out[n]
+    sc_eh.step1c()
+    sc_eo.step1c()
     sc_nh.step3()
     sc_no.step3()
     chan_n0.wait()
@@ -483,22 +616,45 @@
         + mm(slt[...], from_source)
         + mm(dt[...], ch_e[1].reshape(E, LANE))
     )
-    sc_eh.step2()
-    sc_eo.step2()
     chan_e[2].wait()
     ge[...] = ge[...] + ch_e[2].reshape(E, LANE).astype(F32)
+    put_ge = local(ge, ge_hbm, 8)
     for copy in returned:
         copy.wait_recv()
     gl[...] = gl[...] + mm_tn(
         rsel[...].reshape(NN * PER, N), ret_in[...].reshape(NN * PER, LANE)
     )
-    sc_eh.step3()
-    sc_eo.step3()
+    put_gl = local(gl, gl_hbm, 9)
     out_nh[...] = node_scale * sc_nh.finish()
-    out_no[...] = (node_scale * sc_no.finish()).T
-    out_eh[...] = edge_scale * sc_eh.finish()
-    out_eo[...] = (edge_scale * sc_eo.finish()).T
+    out_no[...] = node_scale * sc_no.finish()
+    for step in ("x_step2", "step2", "x_step3", "step3"):
+        for scatter in (sc_eh, sc_eo):
+            getattr(scatter, step)()
+    for scatter, out in ((sc_eh, out_eh), (sc_eo, out_eo)):
+        out[scatter.main:, :] = edge_scale * scatter.x_finish()
+        out[:scatter.main, :] = edge_scale * scatter.finish()
+    put_ge.wait()
+    put_gl.wait()
     flush()
+
+
+def hand_over(*refs):
+    count = (len(refs) - 2) // 3
+    given, taken, held = refs[:count], refs[count:2 * count], refs[2 * count:3 * count]
+    in_sem, out_sem = refs[3 * count:]
+    loads = [
+        pltpu.make_async_copy(a, b, in_sem.at[i]) for i, (a, b) in enumerate(zip(given, held))
+    ]
+    stores = [
+        pltpu.make_async_copy(a, b, out_sem.at[i]) for i, (a, b) in enumerate(zip(held, taken))
+    ]
+    for load in loads:
+        load.start()
+    for load, store in zip(loads, stores):
+        load.wait()
+        store.start()
+    for store in stores:
+        store.wait()
 
 
 def on_device(
@@ -520,15 +676,25 @@
 
     chunks = [3 * L // NN, 2 * L // NN, L // NN, L // NN]
     rs = []
-    for ch in chunks:
+    for i in (0, 3, 1, 2):
+        part = max(16, chunks[i] // 4 // 16 * 16) if i in (0, 3) else 0
+        ch = chunks[i] - part
         rs += [
             v(NZ - 1, NY, ch, HC // 2), v(NY - 1, NZ, ch, HC // 2),
             v(NY, ch, HC // 2), v(NZ, ch, HC // 2),
             v(NY - 1, ch, HC // 2), v(NZ - 1, ch, HC // 2),
             v(ch, HC), v(NX - 1, ch, LANE),
         ]
+        if part:
+            rs += [
+                v(NX - 1, NY, NZ, part, LANE), v(NY, NZ, part, LANE),
+                v(NZ - 1, NY, part, LANE), v(NY, part, LANE), v(NY - 1, part, LANE),
+            ]
     scratch = [
         pltpu.SemaphoreType.DMA((320,)), pltpu.SemaphoreType.DMA((320,)),
+        pltpu.SemaphoreType.DMA((10,)),
+        v(N, LANE), v(E, LANE), v(LANE, L), v(LANE, L), v(N, LANE), v(E, LANE),
+        v(N, LANE, dtype=F32), v(E, LANE, dtype=F32),
         v(3, G, RE, LANE), v(2, G, RN, LANE), v(G, RN, LANE), v(G, RE, LANE),
         v(RE, HC), v(RE, HC, dtype=F32), v(RN, HC, dtype=F32),
         v(E, LANE, dtype=F32), v(E, LANE, dtype=F32), v(E, LANE, dtype=F32),
@@ -544,26 +710,41 @@
     ]
     vmem = pl.BlockSpec(memory_space=pltpu.VMEM)
     smem = pl.BlockSpec(memory_space=pltpu.SMEM)
+    hbm = pl.BlockSpec(memory_space=pl.ANY)
 
     def f(*shape):
         return jax.ShapeDtypeStruct(shape, F32)
 
-    return pl.pallas_call(
+    results = pl.pallas_call(
         functools.partial(kernel, dims),
         out_shape=(
-            f(N, LANE), f(E, LANE), f(chunks[0], LANE), f(LANE, chunks[3]),
-            f(chunks[1], LANE), f(LANE, chunks[2]),
+            f(N, LANE), f(E, LANE), f(chunks[0], LANE), f(chunks[3], LANE),
+            f(chunks[1], LANE), f(chunks[2], LANE),
         ),
-        in_specs=[vmem] * 4 + [smem] + [vmem] * 6,
-        out_specs=[vmem] * 6,
+        in_specs=[hbm, hbm, vmem, vmem, smem] + [hbm] * 6,
+        out_specs=[hbm, hbm] + [vmem] * 4,
         scratch_shapes=scratch,
         compiler_params=pltpu.CompilerParams(
             collective_id=0, has_side_effects=True, vmem_limit_bytes=64 * 1024 * 1024 - 65536
         ),
     )(
-        latents, edge_attr, edge_src.reshape(1, E), edge_dst.reshape(1, E), send_blocks,
-        edge_hidden_w, edge_out_w, node_hidden_w, node_out_w, node_cotangent, edge_cotangent,
+        latents, edge_attr, edge_src, edge_dst, send_blocks[0].T,
+        edge_hidden_w.reshape(NY, NZ, chunks[0], LANE), edge_out_w,
+        node_hidden_w.reshape(NY, NZ, chunks[1], LANE), node_out_w,
+        node_cotangent, edge_cotangent,
     )
+    gl, ge, g_eh, g_eo, g_nh, g_no = pl.pallas_call(
+        hand_over,
+        out_shape=tuple(jax.ShapeDtypeStruct(r.shape, r.dtype) for r in results),
+        in_specs=[hbm] * 6,
+        out_specs=[hbm] * 6,
+        scratch_shapes=[
+            *[pltpu.VMEM(r.shape, r.dtype) for r in results],
+            pltpu.SemaphoreType.DMA((6,)), pltpu.SemaphoreType.DMA((6,)),
+        ],
+        compiler_params=pltpu.CompilerParams(vmem_limit_bytes=60 * 1024 * 1024),
+    )(*results)
+    return gl, ge, g_eh, g_eo.T, g_nh, g_no.T
 
 
 def solution(mesh):

time: 145 us -> 130 us (0.90)
  local copies, waits for them, and re-layouts: 10 us -> 0 us
  Pallas kernels: 134 us -> 129 us
    pallas_call x1, Pallas kernels: 134 us -> 127 us  [on_device(): pl.pallas_call(functools.partial(kernel, dims), out_shape=(f(N, LANE), f(...]
    unnamed x15 -> x0, local copies, waits for them, and re-layouts: 4.99 us -> none
    pallas_call x2 -> x0, local copies, waits for them, and re-layouts: 3.15 us -> none  [on_device(): pl.pallas_call(functools.partial(kernel, dims), out_shape=(f(N, LANE), f(...]
    pallas_call x0 -> x1, Pallas kernels: none -> 2.3 us  [on_device(): pl.pallas_call(hand_over, out_shape=tuple((jax.ShapeDtypeStruct(r.shape,...]
    reshape x2 -> x0, local copies, waits for them, and re-layouts: 1.9 us -> none  [the longest x1 1.3 us: on_device(): edge_src.reshape(1, E)]
where the time goes in v2:
time: 130 us
  Pallas kernels  129 us (99%)
    pallas_call x1, Pallas kernels, on_device(): pl.pallas_call(functools.partial(kernel, dims), out_shape=(f(N, LANE), f(...  127 us

profile of v2, /device:TPU:0, one launch (start us, length us, event | category | flops | bytes accessed | tf_op | source)
XLA Modules:
  0.0 129.9 jit_solution(11499527834960896138)
XLA Ops:
  0.6 126.8 %shard_map.154 = (f32[768,128]{1,0:T(8,128)}, f32[1536,128]{1,0:T(8,128)}, f32[192,128]{1,0:T(8,128)}, f32[64,128]{1,0:T(8,128)}, f32[128,128]{1,0:T(8,128)}, /*index=5*/f32[64,128]{1,0:T(8,128)}) custom-call(bf16[768,128]{1,0:T(8,128)(2,1)} %lat_hbm.1, bf16[1536,128]{1,0:T(8,128)(2,1)} %ea_hbm.1, s32[1536]{0:T(1024)} %src.1, s32[1536]{0:T(1024)} %dst.1, ...), custom_call_target="tpu_custom_call" | custom-call | tf_op jit(solution)/shard_map/pallas_call | solution.py:718
  127.5 2.3 %shard_map.155 = (f32[768,128]{1,0:T(8,128)}, f32[1536,128]{1,0:T(8,128)}, f32[192,128]{1,0:T(8,128)}, f32[64,128]{1,0:T(8,128)}, f32[128,128]{1,0:T(8,128)}, /*index=5*/f32[64,128]{1,0:T(8,128)}) custom-call(f32[768,128]{1,0:T(8,128)} %get-tuple-element.18.refs_0_, f32[1536,128]{1,0:T(8,128)} %get-tuple-element.19.refs_1_, ...), custom_call_target="tpu_custom_call" | custom-call | tf_op jit(solution)/shard_map/pallas_call | solution.py:736

commit v3 on v2

--- a/solution.py
+++ b/solution.py
@@ -260,14 +260,13 @@
                         rcopy(self.g.at[index(1, hi)], land.at[0, hi], peer(1)),
                         rcopy(self.g.at[index(3, lo)], land.at[2, lo], peer(3)),
                     ])
-            if self.over_x:
-                part = pl.ds(self.main, self.g.shape[2] - self.main)
-                self.xs = [
-                    rcopy(
-                        self.g.at[:, :, part, pl.ds(j * LANE, LANE)], self.rx1.at[j - 1], x_peer(j)
-                    )
-                    for j in range(1, NX)
-                ]
+
+        def x_step1(self):
+            part = pl.ds(self.main, self.g.shape[2] - self.main)
+            self.xs = [
+                rcopy(self.g.at[:, :, part, pl.ds(j * LANE, LANE)], self.rx1.at[j - 1], x_peer(j))
+                for j in range(1, NX)
+            ]
 
         def step1c(self):
             for (index, land, size, peer, across), relay, full in zip(
@@ -464,8 +463,6 @@
     gat_eh.step3()
     rows_ea.forward()
     rows_dst.forward()
-    gat_nh.step2()
-    gat_no.step2()
 
     nodes_down = sublane_iota(N)
     for b in range(blocks):
@@ -488,8 +485,6 @@
         )
         srcc[xx] = mm(pick, table).astype(BF)
         rows_src.send(j, srcc.at[xx])
-    gat_nh.step3()
-    gat_no.step3()
     gat_eo.step4()
 
     get_weh.wait()
@@ -498,20 +493,24 @@
     rows_dst.wait()
     weh_all = w_eh[...].reshape(3 * L, HC)
     hpre[...] = mm(wide(ei, (1,)), weh_all[L:2 * L]) + mm(wide(ei, (2,)), weh_all[2 * L:])
+    gat_nh.step2()
+    gat_no.step2()
     rows_src.forward()
     get_nct.wait()
     rows_lat = ToRows(lambda g: ni.at[0, g]).send_all(lambda xx: lat.at[pl.ds(xx * RN, RN), :])
     rows_cot = ToRows(lambda g: cot.at[g]).send_all(lambda xx: nct.at[pl.ds(xx * RN, RN), :])
-    gat_nh.step4()
-    gat_no.step4()
     rows_src.wait()
     pre = hpre[...] + mm(wide(ei, (0,)), weh_all[:L])
     hpre[...] = pre
     hidden[...] = (pre * jax.nn.sigmoid(pre)).astype(BF)
+    gat_nh.step3()
+    gat_no.step3()
     gat_eo.wait()
     weo_all = w_eo[...].reshape(L, HC)
     chan_m = ToChan(mm_nt(hidden[...], weo_all), pb_m, rx_m, ch_m)
     chan_m.forward()
+    gat_nh.step4()
+    gat_no.step4()
     rows_lat.forward()
     rows_cot.forward()
     chan_m.wait()
@@ -546,8 +545,8 @@
             part = mm_tn(values[:, yy * per_y:(yy + 1) * per_y], back)
             g[yy] = part.astype(BF).reshape(g.shape[1:])
 
-    sc_eh, sc_eo = Scatter(g_eh, rs_bufs[0:13], True), Scatter(g_eo, rs_bufs[13:26], True)
-    sc_nh, sc_no = Scatter(g_nh, rs_bufs[26:34]), Scatter(g_no, rs_bufs[34:42])
+    sc_eh, sc_eo = Scatter(g_eh, rs_bufs[0:13], True), Scatter(g_eo, rs_bufs[13:21])
+    sc_nh, sc_no = Scatter(g_nh, rs_bufs[21:29]), Scatter(g_no, rs_bufs[29:37])
     weight_grad(g_nh, jnp.concatenate([wide(ni, (0,)), wide(ni, (1,))], axis=1), node_back)
     sc_nh.step1()
     weight_grad(g_no, cots, node_hidden)
@@ -575,25 +574,27 @@
     rows_mg.wait()
     message_grad = wide(mg)
     edge_back = (mm(message_grad, weo_all) * hpre[...]).astype(BF)
-    chan_e = [
-        ToChan(
+    def pull(t):
+        return ToChan(
             mm_nt(edge_back, weh_all[t * L:(t + 1) * L]), pb_e.at[t], rx_e.at[t], ch_e.at[t]
         )
-        for t in range(3)
-    ]
-    chan_e[0].forward()
+
+    chan_e = [pull(0)]
     weight_grad(
         g_eh, jnp.concatenate([wide(ei, (t,)) for t in range(3)], axis=1), edge_back
     )
     sc_eh.step1()
+    chan_e[0].forward()
+    sc_eh.step1b()
+    chan_e += [pull(1), pull(2)]
     chan_e[1].forward()
     weight_grad(g_eo, message_grad, hidden[...])
     sc_eo.step1()
+    chan_e[2].forward()
+    sc_eo.step1b()
+    sc_eh.x_step1()
     sc_nh.step2()
     sc_no.step2()
-    chan_e[2].forward()
-    sc_eh.step1b()
-    sc_eo.step1b()
 
     chan_e[0].wait()
     from_source = ch_e[0].reshape(E, LANE)
@@ -627,12 +628,15 @@
     put_gl = local(gl, gl_hbm, 9)
     out_nh[...] = node_scale * sc_nh.finish()
     out_no[...] = node_scale * sc_no.finish()
-    for step in ("x_step2", "step2", "x_step3", "step3"):
-        for scatter in (sc_eh, sc_eo):
-            getattr(scatter, step)()
-    for scatter, out in ((sc_eh, out_eh), (sc_eo, out_eo)):
-        out[scatter.main:, :] = edge_scale * scatter.x_finish()
-        out[:scatter.main, :] = edge_scale * scatter.finish()
+    sc_eh.step2()
+    sc_eo.step2()
+    sc_eh.x_step2()
+    sc_eh.step3()
+    sc_eo.step3()
+    sc_eh.x_step3()
+    out_eh[:sc_eh.main, :] = edge_scale * sc_eh.finish()
+    out_eo[...] = edge_scale * sc_eo.finish()
+    out_eh[sc_eh.main:, :] = edge_scale * sc_eh.x_finish()
     put_ge.wait()
     put_gl.wait()
     flush()
@@ -677,7 +681,7 @@
     chunks = [3 * L // NN, 2 * L // NN, L // NN, L // NN]
     rs = []
     for i in (0, 3, 1, 2):
-        part = max(16, chunks[i] // 4 // 16 * 16) if i in (0, 3) else 0
+        part = max(16, chunks[i] // 6 // 16 * 16) if i == 0 else 0
         ch = chunks[i] - part
         rs += [
             v(NZ - 1, NY, ch, HC // 2), v(NY - 1, NZ, ch, HC // 2),

time: 130 us -> 120 us (0.923)
  Pallas kernels: 129 us -> 119 us
    pallas_call x1, Pallas kernels: 127 us -> 117 us  [on_device(): pl.pallas_call(functools.partial(kernel, dims), out_shape=(f(N, LANE), f(...]
where the time goes in v3:
time: 120 us
  Pallas kernels  119 us (99%)
    pallas_call x1, Pallas kernels, on_device(): pl.pallas_call(functools.partial(kernel, dims), out_shape=(f(N, LANE), f(...  117 us

profile of v3, /device:TPU:0, one launch (start us, length us, event | category | flops | bytes accessed | tf_op | source)
XLA Modules:
  0.0 120.1 jit_solution(2877217302078371)
XLA Ops:
  0.6 117.0 %shard_map.154 = (f32[768,128]{1,0:T(8,128)}, f32[1536,128]{1,0:T(8,128)}, f32[192,128]{1,0:T(8,128)}, f32[64,128]{1,0:T(8,128)}, f32[128,128]{1,0:T(8,128)}, /*index=5*/f32[64,128]{1,0:T(8,128)}) custom-call(bf16[768,128]{1,0:T(8,128)(2,1)} %lat_hbm.1, bf16[1536,128]{1,0:T(8,128)(2,1)} %ea_hbm.1, s32[1536]{0:T(1024)} %src.1, s32[1536]{0:T(1024)} %dst.1, ...), custom_call_target="tpu_custom_call" | custom-call | tf_op jit(solution)/shard_map/pallas_call | solution.py:722
  117.7 2.3 %shard_map.155 = (f32[768,128]{1,0:T(8,128)}, f32[1536,128]{1,0:T(8,128)}, f32[192,128]{1,0:T(8,128)}, f32[64,128]{1,0:T(8,128)}, f32[128,128]{1,0:T(8,128)}, /*index=5*/f32[64,128]{1,0:T(8,128)}) custom-call(f32[768,128]{1,0:T(8,128)} %get-tuple-element.18.refs_0_, f32[1536,128]{1,0:T(8,128)} %get-tuple-element.19.refs_1_, ...), custom_call_target="tpu_custom_call" | custom-call | tf_op jit(solution)/shard_map/pallas_call | solution.py:740

commit v4 on v3

--- a/solution.py
+++ b/solution.py
@@ -421,6 +421,9 @@
 
     gat_eh, gat_nh, gat_no, gat_eo = Gather(w_eh), Gather(w_nh), Gather(w_no), Gather(w_eo)
     gat_eh.step1(weh.at[y, z])
+    gat_eo.step1(w_eo.at[y, z, :, pl.ds(0, LANE)])
+    gat_nh.step1(wnh.at[y, z])
+    gat_no.step1(w_no.at[y, z, :, pl.ds(0, LANE)])
     ask = [
         rcopy(rq_out.at[(n + j) % NN], rq_in.at[n], n_peer(j)) for j in range(1, NN)
     ]
@@ -428,9 +431,6 @@
     get_lat.wait()
     get_ea.wait()
     rows_ea = ToRows(lambda g: ei.at[2, g]).send_all(lambda xx: ea.at[pl.ds(xx * RE, RE), :])
-    gat_eo.step1(w_eo.at[y, z, :, pl.ds(0, LANE)])
-    gat_nh.step1(wnh.at[y, z])
-    gat_no.step1(w_no.at[y, z, :, pl.ds(0, LANE)])
 
     rows_dst = ToRows(lambda g: ei.at[1, g])
     for j in [*far_first, 0]:

time: 120 us -> 119 us (level)
  no operation moved by 1% of the time
where the time goes in v4:
time: 119 us
  Pallas kernels  119 us (100%)
    pallas_call x1, Pallas kernels, on_device(): pl.pallas_call(functools.partial(kernel, dims), out_shape=(f(N, LANE), f(...  116 us

profile of v4, /device:TPU:0, one launch (start us, length us, event | category | flops | bytes accessed | tf_op | source)
XLA Modules:
  0.0 119.3 jit_solution(1567360217356970969)
XLA Ops:
  0.6 116.2 %shard_map.154 = (f32[768,128]{1,0:T(8,128)}, f32[1536,128]{1,0:T(8,128)}, f32[192,128]{1,0:T(8,128)}, f32[64,128]{1,0:T(8,128)}, f32[128,128]{1,0:T(8,128)}, /*index=5*/f32[64,128]{1,0:T(8,128)}) custom-call(bf16[768,128]{1,0:T(8,128)(2,1)} %lat_hbm.1, bf16[1536,128]{1,0:T(8,128)(2,1)} %ea_hbm.1, s32[1536]{0:T(1024)} %src.1, s32[1536]{0:T(1024)} %dst.1, ...), custom_call_target="tpu_custom_call" | custom-call | tf_op jit(solution)/shard_map/pallas_call | solution.py:722
  116.8 2.3 %shard_map.155 = (f32[768,128]{1,0:T(8,128)}, f32[1536,128]{1,0:T(8,128)}, f32[192,128]{1,0:T(8,128)}, f32[64,128]{1,0:T(8,128)}, f32[128,128]{1,0:T(8,128)}, /*index=5*/f32[64,128]{1,0:T(8,128)}) custom-call(f32[768,128]{1,0:T(8,128)} %get-tuple-element.18.refs_0_, f32[1536,128]{1,0:T(8,128)} %get-tuple-element.19.refs_1_, ...), custom_call_target="tpu_custom_call" | custom-call | tf_op jit(solution)/shard_map/pallas_call | solution.py:740

commit v5 on v4

--- a/solution.py
+++ b/solution.py
@@ -110,8 +110,8 @@
         pending.append(copy)
         return copy
 
-    def flush():
-        while pending:
+    def flush(count):
+        for _ in range(count):
             pending.pop(0).wait_send()
 
     far_first = sorted(range(1, NX), key=lambda j: -min(j, NX - j))
@@ -440,6 +440,7 @@
         rows_dst.send(j, dstc.at[xx])
 
     gat_eh.step2()
+    gat_eo.step2()
 
     for copy in ask:
         copy.wait_recv()
@@ -459,7 +460,6 @@
     ]
     row_in[n] = row_out[n]
 
-    gat_eo.step2()
     gat_eh.step3()
     rows_ea.forward()
     rows_dst.forward()
@@ -548,6 +548,7 @@
     sc_eh, sc_eo = Scatter(g_eh, rs_bufs[0:13], True), Scatter(g_eo, rs_bufs[13:21])
     sc_nh, sc_no = Scatter(g_nh, rs_bufs[21:29]), Scatter(g_no, rs_bufs[29:37])
     weight_grad(g_nh, jnp.concatenate([wide(ni, (0,)), wide(ni, (1,))], axis=1), node_back)
+    settled = len(pending)
     sc_nh.step1()
     weight_grad(g_no, cots, node_hidden)
     sc_no.step1()
@@ -593,6 +594,7 @@
     chan_e[2].forward()
     sc_eo.step1b()
     sc_eh.x_step1()
+    flush(settled)
     sc_nh.step2()
     sc_no.step2()
 
@@ -639,7 +641,7 @@
     out_eh[sc_eh.main:, :] = edge_scale * sc_eh.x_finish()
     put_ge.wait()
     put_gl.wait()
-    flush()
+    flush(len(pending))
 
 
 def hand_over(*refs):

time: 119 us -> 119 us (level)
  no operation moved by 1% of the time
where the time goes in v5:
time: 119 us
  Pallas kernels  118 us (99%)
    pallas_call x1, Pallas kernels, on_device(): pl.pallas_call(functools.partial(kernel, dims), out_shape=(f(N, LANE), f(...  116 us

profile of v5, /device:TPU:0, one launch (start us, length us, event | category | flops | bytes accessed | tf_op | source)
XLA Modules:
  0.0 118.6 jit_solution(1221088088748613786)
XLA Ops:
  0.6 115.5 %shard_map.154 = (f32[768,128]{1,0:T(8,128)}, f32[1536,128]{1,0:T(8,128)}, f32[192,128]{1,0:T(8,128)}, f32[64,128]{1,0:T(8,128)}, f32[128,128]{1,0:T(8,128)}, /*index=5*/f32[64,128]{1,0:T(8,128)}) custom-call(bf16[768,128]{1,0:T(8,128)(2,1)} %lat_hbm.1, bf16[1536,128]{1,0:T(8,128)(2,1)} %ea_hbm.1, s32[1536]{0:T(1024)} %src.1, s32[1536]{0:T(1024)} %dst.1, ...), custom_call_target="tpu_custom_call" | custom-call | tf_op jit(solution)/shard_map/pallas_call | solution.py:724
  116.2 2.3 %shard_map.155 = (f32[768,128]{1,0:T(8,128)}, f32[1536,128]{1,0:T(8,128)}, f32[192,128]{1,0:T(8,128)}, f32[64,128]{1,0:T(8,128)}, f32[128,128]{1,0:T(8,128)}, /*index=5*/f32[64,128]{1,0:T(8,128)}) custom-call(f32[768,128]{1,0:T(8,128)} %get-tuple-element.18.refs_0_, f32[1536,128]{1,0:T(8,128)} %get-tuple-element.19.refs_1_, ...), custom_call_target="tpu_custom_call" | custom-call | tf_op jit(solution)/shard_map/pallas_call | solution.py:742
